TPU v7x, 32 devices: a whole 2x2x4 slice. The times are simulated.
32 devices in a mesh: groups: 2 (over y), wide: 4 (over z), narrow: 2 (over x), vec: 2 (over core).
Axes of the slice: x: 2, y: 2, z: 4, core: 2. Of those that a mesh axis runs over, the one named last changes fastest.
Arguments:
- vectors: float32 [128, 128, 256], P(('groups', 'wide', 'narrow'), None, 'vec'), parts along dimension 0, may hold values from -6 to 6
- points: bfloat16 [128, 3, 256], P(('groups', 'wide', 'narrow')), parts along dimension 0, may hold values from 0 to 1
- near_list: int32 [128, 16], P(('groups', 'wide', 'narrow')), parts along dimension 0, may hold values from -1 to 63, as said below
- leaf_basis: bfloat16 [128, 64, 256], P(('groups', 'wide', 'narrow'), None, 'vec'), parts along dimension 0, may hold values from -0.375 to 0.375
- leaf_transfer: float32 [128, 64, 64], P(('groups', 'wide', 'narrow')), parts along dimension 0, may hold values from -0.75 to 0.75
- parent_to_cluster: float32 [16, 64, 64], P(('groups', 'wide', 'narrow')), parts along dimension 0, may hold values from -0.75 to 0.75
- skeleton: float32 [8, 3, 64], P('groups'), parts along dimension 0, may hold values from 0 to 1
- coupling: int32 [8, 2], P(('groups', 'wide')), parts along dimension 0, may hold values from 0 to 3, as said below
Outputs:
- product: float32 [128, 128, 256], P(('groups', 'wide', 'narrow'), None, 'vec'), parts along dimension 0
There are 2 independent parts, one for each index of `groups`. A program takes and returns all parts, laid end to end along the dimension named above; each array names one. Nothing has to cross between parts.
Inputs may be any that keep to these rules, and one draw needn't show every extreme that they name: `near_list`: entry 0 of a row is the row's own leaf; the used entries of a row are distinct leaves, at least two, and -1 fills the unused slots after them. Among the rows of one device (aligned blocks of 8 rows), at most 4 distinct leaves lie in any one other cluster of 16 leaves, and every device reaches 4 for some cluster. `coupling`: each row names 2 distinct clusters other than its own.
All inputs are finite; a program needn't handle non-finite values.
Results may differ from a plain program's by a relative error of at most 0.0045.
Values may be sent and summed in bfloat16 or wider, within the bound.
A program may use at most 64 MiB of HBM per device.

v0:
```python
import jax
import jax.numpy as jnp
from jax import lax
from jax.sharding import PartitionSpec as P

SEND_CAP = 4


kernel_rate = 8.660254037844386
signal = 0.125
finest_level = lax.Precision.HIGHEST


def matern_kernel(source_pts, target_pts):
    first = source_pts.astype(jnp.float32)
    second = target_pts.astype(jnp.float32)
    delta_x = first[..., 0, :, None] - second[..., 0, None, :]
    delta_y = first[..., 1, :, None] - second[..., 1, None, :]
    delta_z = first[..., 2, :, None] - second[..., 2, None, :]
    squared = delta_x * delta_x + delta_y * delta_y + delta_z * delta_z
    scaled = kernel_rate * jnp.sqrt(squared)
    return signal * (1.0 + scaled) * jnp.exp(-scaled)


def body(
    vectors, points, near_list, leaf_basis, leaf_transfer, parent_to_cluster, skeleton, coupling
):
    block_count = lax.axis_size("wide")
    narrow_count = lax.axis_size("narrow")
    wide_pos = lax.axis_index("wide")
    vec_pos = lax.axis_index("vec")
    leaf_dev, columns, half_points = vectors.shape
    full_points = points.shape[2]
    block_len = leaf_dev * narrow_count
    slot_total = near_list.shape[1]
    x_width = columns * half_points
    pts_width = 3 * full_points
    rounded = vectors.astype(jnp.bfloat16)
    block_x, block_pts = (
        lax.all_gather(rounded, "narrow", axis=0, tiled=True),
        lax.all_gather(points, "narrow", axis=0, tiled=True),
    )
    block_flat = jnp.concatenate(
        [block_x.reshape(block_len, x_width), block_pts.reshape(block_len, pts_width)], axis=1
    )
    flat_entries = near_list.reshape(-1)
    usable_flat = flat_entries >= 0
    clamped_flat = jnp.maximum(flat_entries, 0)
    matches = (clamped_flat[:, None] == jnp.arange(block_count * block_len)[None, :]) & usable_flat[
        :, None
    ]
    needed = jnp.max(matches.astype(jnp.int32), axis=0).reshape(block_count, block_len)
    needed = needed * (jnp.arange(block_count) != wide_pos).astype(jnp.int32)[:, None]
    requested = lax.all_to_all(needed, "wide", split_axis=0, concat_axis=0, tiled=True)
    requested_rank = jnp.cumsum(requested, axis=1) - 1
    selected_option = (requested[:, None, :] == 1) & (
        requested_rank[:, None, :] == jnp.arange(SEND_CAP)[None, :, None]
    )
    send_picked = jnp.einsum(
        "gsb,bw->gsw",
        selected_option.astype(jnp.bfloat16),
        block_flat,
        preferred_element_type=jnp.float32,
    ).astype(jnp.bfloat16)
    send_x = send_picked[:, :, :x_width].reshape(block_count, SEND_CAP, columns, half_points)
    send_pts = send_picked[:, :, x_width:].reshape(block_count, SEND_CAP, 3, full_points)
    recv_x, recv_pts = (
        lax.all_to_all(send_x, "wide", split_axis=0, concat_axis=0, tiled=True),
        lax.all_to_all(send_pts, "wide", split_axis=0, concat_axis=0, tiled=True),
    )
    recv_flat = jnp.concatenate(
        [
            recv_x.reshape(block_count * SEND_CAP, x_width),
            recv_pts.reshape(block_count * SEND_CAP, pts_width),
        ],
        axis=1,
    )
    candidates = jnp.concatenate([block_flat, recv_flat], axis=0)
    cand_total = candidates.shape[0]
    needed_rank = (jnp.cumsum(needed, axis=1) - 1).reshape(-1)
    leaf_range = jnp.arange(block_count * block_len)

    def locate(slot_index):
        entries = lax.dynamic_index_in_dim(near_list, slot_index, 1, keepdims=False)
        usable = (entries >= 0).astype(jnp.float32)
        clamped = jnp.maximum(entries, 0)
        owner_block = clamped // block_len
        inner_index = clamped % block_len
        is_local = owner_block == wide_pos
        rank_found = jnp.sum(
            (clamped[:, None] == leaf_range[None, :]).astype(jnp.int32) * needed_rank[None, :],
            axis=1,
        )
        recv_slot = jnp.maximum(owner_block * SEND_CAP + rank_found, 0)
        chosen = jnp.where(is_local, inner_index, block_len + recv_slot)
        one_hot = (chosen[:, None] == jnp.arange(cand_total)[None, :]).astype(jnp.bfloat16)
        picked = jnp.dot(one_hot, candidates, preferred_element_type=jnp.float32).astype(
            jnp.bfloat16
        )
        sources = picked[:, :x_width].reshape(leaf_dev, columns, half_points)
        source_pts = picked[:, x_width:].reshape(leaf_dev, 3, full_points)
        return (usable, sources, source_pts)

    def scatter_step(slot_index, running):
        usable, sources, source_pts = locate(slot_index)
        source_half = lax.dynamic_slice_in_dim(source_pts, vec_pos * half_points, half_points, 2)
        kernel_tile = matern_kernel(source_half, points) * usable[:, None, None]
        return running + jnp.einsum(
            "mkp,mpj->mkj",
            sources,
            kernel_tile.astype(jnp.bfloat16),
            preferred_element_type=jnp.float32,
        )

    partial_near = lax.fori_loop(
        0, slot_total, scatter_step, jnp.zeros((leaf_dev, columns, full_points), jnp.float32)
    )
    near_part = lax.psum_scatter(
        partial_near.astype(jnp.bfloat16), "vec", scatter_dimension=2, tiled=True
    ).astype(jnp.float32)
    leaf_weights = jnp.einsum(
        "lcp,lrp->lcr", rounded, leaf_basis, preferred_element_type=jnp.float32
    )
    parent_weight_sums = jnp.einsum(
        "lcr,lrq->cq", leaf_weights, leaf_transfer, precision=finest_level
    )
    parent_term = jnp.dot(parent_weight_sums, parent_to_cluster[0], precision=finest_level)
    placed = (jnp.arange(block_count) == wide_pos).astype(jnp.float32)[:, None, None] * parent_term[
        None
    ]
    root_weight_values = lax.psum(placed, ("wide", "narrow", "vec"))
    partners = coupling[0]
    sources_top = jnp.take(root_weight_values, partners, axis=0)
    own_skeleton = lax.dynamic_index_in_dim(skeleton, wide_pos, 0, keepdims=True)
    coupling_tile = matern_kernel(jnp.take(skeleton, partners, axis=0), own_skeleton)
    top_fields = jnp.einsum("kcr,krq->cq", sources_top, coupling_tile, precision=finest_level)
    parent_fields = jnp.einsum(
        "cq,rq->cr", top_fields, parent_to_cluster[0], precision=finest_level
    )
    leaf_fields = jnp.einsum(
        "cq,lrq->lcr", parent_fields, leaf_transfer, precision=finest_level
    ).astype(jnp.bfloat16)
    far_part = jnp.einsum(
        "lcr,lrp->lcp", leaf_fields, leaf_basis, preferred_element_type=jnp.float32
    )
    return vectors + near_part + far_part


def solution(mesh):
    in_specs = (
        P(("groups", "wide", "narrow"), None, "vec"),
        P(("groups", "wide", "narrow"), None, None),
        P(("groups", "wide", "narrow"), None),
        P(("groups", "wide", "narrow"), None, "vec"),
        P(("groups", "wide", "narrow"), None, None),
        P(("groups", "wide", "narrow"), None, None),
        P("groups", None, None),
        P(("groups", "wide"), None),
    )
    out_specs = P(("groups", "wide", "narrow"), None, "vec")
    return jax.shard_map(body, mesh=mesh, in_specs=in_specs, out_specs=out_specs, check_vma=False)
```

profile of v0, /device:TPU:0, one launch (start us, length us, event | category | flops | bytes accessed | tf_op | source)
XLA Modules:
  0.0 143.2 jit_solution(196887545797347343)
XLA Ops:
  7.4 0.7 broadcast_compare_fusion
  8.1 0.7 broadcast_maximum_fusion
  9.2 0.7 broadcast_multiply_fusion.1
  9.8 6.3 %all-to-all-start = ((s32[4,1,16]{2,1,0:T(1,128)}), s32[4,1,16]{2,1,0:T(1,128)S(1)}, u32[]{:S(2)}, u32[]{:S(2)}) async-start(s32[4,1,16]{2,1,0:T(1,128)} %bitcast), calls=%async_computation | async-start | bytes 4096 | tf_op jit(solution)/shard_map/all_to_all | solution.py:54
  16.2 4.6 %all_gather.7 = bf16[16,3,256]{2,0,1:T(8,128)(2,1)S(1)} all-gather(bf16[8,3,256]{2,0,1:T(8,128)(2,1)} %param.11), channel_id=1, replica_groups=mesh['groups'=2,'wide'=4,'narrow'=2,'vec'=2] {'narrow'}, dimensions={0}, use_global_device_ids=true | all-gather | bytes 36864 | tf_op jit(solution)/shard_map/all_gather | solution.py:41
  20.8 1.1 convert_element_type.101
  21.8 7.3 %all_gather.6 = bf16[16,128,128]{2,1,0:T(8,128)(2,1)S(1)} all-gather(bf16[8,128,128]{2,1,0:T(8,128)(2,1)S(1)} %convert_element_type.101), channel_id=1, replica_groups=mesh['groups'=2,'wide'=4,'narrow'=2,'vec'=2] {'narrow'}, dimensions={0}, use_global_device_ids=true | all-gather | bytes 786432 | tf_op jit(solution)/shard_map/all_gather | solution.py:40
  29.1 0.3 fusion.66
  29.4 0.3 bitcast_dynamic-update-slice_fusion
  29.8 0.6 convolution_bitcast_fusion.2
  30.4 0.2 fusion.40
  30.9 0.3 convolution_convert_fusion.1
  31.2 0.6 slice.133
  31.8 4.8 %all-to-all-start.2 = ((bf16[4,4,3,256]{3,1,2,0:T(4,128)(2,1)}), bf16[4,4,3,256]{3,1,2,0:T(4,128)(2,1)S(1)}, u32[]{:S(2)}, u32[]{:S(2)}) async-start(bf16[4,4,3,256]{3,1,2,0:T(4,128)(2,1)} %bitcast.3), calls=%async_computation.2 | async-start | bytes 49152 | tf_op jit(solution)/shard_map/all_to_all | solution.py:69
  36.6 0.7 broadcast_multiply_fusion
  37.7 1.3 reshape.174
  39.1 3.2 %all-to-all-done.2 = bf16[4,4,3,256]{3,1,2,0:T(4,128)(2,1)S(1)} async-done(((bf16[4,4,3,256]{3,1,2,0:T(4,128)(2,1)}), bf16[4,4,3,256]{3,1,2,0:T(4,128)(2,1)S(1)}, u32[]{:S(2)}, u32[]{:S(2)}) %all-to-all-start.2) | async-done | bytes 24608 | tf_op jit(solution)/shard_map/all_to_all | solution.py:69
  42.3 3.5 %all-to-all-start.1 = ((bf16[4,4,128,128]{3,2,1,0:T(8,128)(2,1)}), bf16[4,4,128,128]{3,2,1,0:T(8,128)(2,1)S(1)}, u32[]{:S(2)}, u32[]{:S(2)}) async-start(bf16[4,4,128,128]{3,2,1,0:T(8,128)(2,1)} %reshape.174), calls=%async_computation.1 | async-start | bytes 1048576 | tf_op jit(solution)/shard_map/all_to_all | solution.py:68
  46.2 10.4 %all-to-all-done.1 = bf16[4,4,128,128]{3,2,1,0:T(8,128)(2,1)S(1)} async-done(((bf16[4,4,128,128]{3,2,1,0:T(8,128)(2,1)}), bf16[4,4,128,128]{3,2,1,0:T(8,128)(2,1)S(1)}, u32[]{:S(2)}, u32[]{:S(2)}) %all-to-all-start.1) | async-done | bytes 524320 | tf_op jit(solution)/shard_map/all_to_all | solution.py:68
  56.6 0.3 copy.52
  57.0 0.6 copy-done.3
  57.6 40.4 %while.17 = (s32[]{:T(128)}, f32[8,128,256]{2,1,0:T(8,128)S(1)}, s32[8,16]{0,1:T(8,128)S(1)}, s32[]{:T(128)}, s32[4,16]{1,0:T(4,128)}, /*index=5*/bf16[32,17152]...) while((s32[]{:T(128)}, f32[8,128,256]{2,1,0:T(8,128)S(1)}, ...), condition=%wide.wide.region_5.6_spmd.clone, body=%wide.wide.region_3.5_spmd.clone.sunk | while | flops 80495528 | bytes 4446963 | solution.py:115
  57.9 0.3 convolution_convert_fusion.5
  58.3 1.8 %convolution_add_fusion.4 = f32[8,128,256]{2,1,0:T(8,128)S(1)} fusion(f32[8,128,256]{2,1,0:T(8,128)S(1)} %get-tuple-element.448, f32[8]{0:T(128)S(1)} %fusion.88, f32[8,256]{1,0:T(8,128)S(1)} %get-tuple-element.430, f32[8,128]{1,0:T(8,128)S(1)} %get-tuple-element.431, f32[8,256]{1,0:T(8,128)S(1)} %get-tuple-element.432, ...), kind=kOutput, calls=%fused_computation.4.clone.clone.1 | convolution fusion | flops 71565312 | bytes 2396193 | tf_op jit(solution)/shard_map/while/body/eval_jaxpr/mkp,mpj->mkj/dot_general | solution.py:108
  60.4 0.3 convolution_convert_fusion.5
  60.8 1.8 %convolution_add_fusion.4 = f32[8,128,256]{2,1,0:T(8,128)S(1)} fusion(f32[8,128,256]{2,1,0:T(8,128)S(1)} %get-tuple-element.448, f32[8]{0:T(128)S(1)} %fusion.88, f32[8,256]{1,0:T(8,128)S(1)} %get-tuple-element.430, f32[8,128]{1,0:T(8,128)S(1)} %get-tuple-element.431, f32[8,256]{1,0:T(8,128)S(1)} %get-tuple-element.432, ...), kind=kOutput, calls=%fused_computation.4.clone.clone.1 | convolution fusion | flops 71565312 | bytes 2396193 | tf_op jit(solution)/shard_map/while/body/eval_jaxpr/mkp,mpj->mkj/dot_general | solution.py:108
  63.0 0.3 convolution_convert_fusion.5
  63.4 1.8 %convolution_add_fusion.4 = f32[8,128,256]{2,1,0:T(8,128)S(1)} fusion(f32[8,128,256]{2,1,0:T(8,128)S(1)} %get-tuple-element.448, f32[8]{0:T(128)S(1)} %fusion.88, f32[8,256]{1,0:T(8,128)S(1)} %get-tuple-element.430, f32[8,128]{1,0:T(8,128)S(1)} %get-tuple-element.431, f32[8,256]{1,0:T(8,128)S(1)} %get-tuple-element.432, ...), kind=kOutput, calls=%fused_computation.4.clone.clone.1 | convolution fusion | flops 71565312 | bytes 2396193 | tf_op jit(solution)/shard_map/while/body/eval_jaxpr/mkp,mpj->mkj/dot_general | solution.py:108
  65.5 0.3 convolution_convert_fusion.5
  65.9 1.8 %convolution_add_fusion.4 = f32[8,128,256]{2,1,0:T(8,128)S(1)} fusion(f32[8,128,256]{2,1,0:T(8,128)S(1)} %get-tuple-element.448, f32[8]{0:T(128)S(1)} %fusion.88, f32[8,256]{1,0:T(8,128)S(1)} %get-tuple-element.430, f32[8,128]{1,0:T(8,128)S(1)} %get-tuple-element.431, f32[8,256]{1,0:T(8,128)S(1)} %get-tuple-element.432, ...), kind=kOutput, calls=%fused_computation.4.clone.clone.1 | convolution fusion | flops 71565312 | bytes 2396193 | tf_op jit(solution)/shard_map/while/body/eval_jaxpr/mkp,mpj->mkj/dot_general | solution.py:108
  68.0 0.3 convolution_convert_fusion.5
  68.4 1.8 %convolution_add_fusion.4 = f32[8,128,256]{2,1,0:T(8,128)S(1)} fusion(f32[8,128,256]{2,1,0:T(8,128)S(1)} %get-tuple-element.448, f32[8]{0:T(128)S(1)} %fusion.88, f32[8,256]{1,0:T(8,128)S(1)} %get-tuple-element.430, f32[8,128]{1,0:T(8,128)S(1)} %get-tuple-element.431, f32[8,256]{1,0:T(8,128)S(1)} %get-tuple-element.432, ...), kind=kOutput, calls=%fused_computation.4.clone.clone.1 | convolution fusion | flops 71565312 | bytes 2396193 | tf_op jit(solution)/shard_map/while/body/eval_jaxpr/mkp,mpj->mkj/dot_general | solution.py:108
  70.5 0.3 convolution_convert_fusion.5
  70.9 1.8 %convolution_add_fusion.4 = f32[8,128,256]{2,1,0:T(8,128)S(1)} fusion(f32[8,128,256]{2,1,0:T(8,128)S(1)} %get-tuple-element.448, f32[8]{0:T(128)S(1)} %fusion.88, f32[8,256]{1,0:T(8,128)S(1)} %get-tuple-element.430, f32[8,128]{1,0:T(8,128)S(1)} %get-tuple-element.431, f32[8,256]{1,0:T(8,128)S(1)} %get-tuple-element.432, ...), kind=kOutput, calls=%fused_computation.4.clone.clone.1 | convolution fusion | flops 71565312 | bytes 2396193 | tf_op jit(solution)/shard_map/while/body/eval_jaxpr/mkp,mpj->mkj/dot_general | solution.py:108
  73.1 0.3 convolution_convert_fusion.5
  73.5 1.8 %convolution_add_fusion.4 = f32[8,128,256]{2,1,0:T(8,128)S(1)} fusion(f32[8,128,256]{2,1,0:T(8,128)S(1)} %get-tuple-element.448, f32[8]{0:T(128)S(1)} %fusion.88, f32[8,256]{1,0:T(8,128)S(1)} %get-tuple-element.430, f32[8,128]{1,0:T(8,128)S(1)} %get-tuple-element.431, f32[8,256]{1,0:T(8,128)S(1)} %get-tuple-element.432, ...), kind=kOutput, calls=%fused_computation.4.clone.clone.1 | convolution fusion | flops 71565312 | bytes 2396193 | tf_op jit(solution)/shard_map/while/body/eval_jaxpr/mkp,mpj->mkj/dot_general | solution.py:108
  75.6 0.3 convolution_convert_fusion.5
  76.0 1.8 %convolution_add_fusion.4 = f32[8,128,256]{2,1,0:T(8,128)S(1)} fusion(f32[8,128,256]{2,1,0:T(8,128)S(1)} %get-tuple-element.448, f32[8]{0:T(128)S(1)} %fusion.88, f32[8,256]{1,0:T(8,128)S(1)} %get-tuple-element.430, f32[8,128]{1,0:T(8,128)S(1)} %get-tuple-element.431, f32[8,256]{1,0:T(8,128)S(1)} %get-tuple-element.432, ...), kind=kOutput, calls=%fused_computation.4.clone.clone.1 | convolution fusion | flops 71565312 | bytes 2396193 | tf_op jit(solution)/shard_map/while/body/eval_jaxpr/mkp,mpj->mkj/dot_general | solution.py:108
  78.1 0.3 convolution_convert_fusion.5
  78.5 1.8 %convolution_add_fusion.4 = f32[8,128,256]{2,1,0:T(8,128)S(1)} fusion(f32[8,128,256]{2,1,0:T(8,128)S(1)} %get-tuple-element.448, f32[8]{0:T(128)S(1)} %fusion.88, f32[8,256]{1,0:T(8,128)S(1)} %get-tuple-element.430, f32[8,128]{1,0:T(8,128)S(1)} %get-tuple-element.431, f32[8,256]{1,0:T(8,128)S(1)} %get-tuple-element.432, ...), kind=kOutput, calls=%fused_computation.4.clone.clone.1 | convolution fusion | flops 71565312 | bytes 2396193 | tf_op jit(solution)/shard_map/while/body/eval_jaxpr/mkp,mpj->mkj/dot_general | solution.py:108
  80.7 0.3 convolution_convert_fusion.5
  81.0 1.8 %convolution_add_fusion.4 = f32[8,128,256]{2,1,0:T(8,128)S(1)} fusion(f32[8,128,256]{2,1,0:T(8,128)S(1)} %get-tuple-element.448, f32[8]{0:T(128)S(1)} %fusion.88, f32[8,256]{1,0:T(8,128)S(1)} %get-tuple-element.430, f32[8,128]{1,0:T(8,128)S(1)} %get-tuple-element.431, f32[8,256]{1,0:T(8,128)S(1)} %get-tuple-element.432, ...), kind=kOutput, calls=%fused_computation.4.clone.clone.1 | convolution fusion | flops 71565312 | bytes 2396193 | tf_op jit(solution)/shard_map/while/body/eval_jaxpr/mkp,mpj->mkj/dot_general | solution.py:108
  83.2 0.3 convolution_convert_fusion.5
  83.6 1.8 %convolution_add_fusion.4 = f32[8,128,256]{2,1,0:T(8,128)S(1)} fusion(f32[8,128,256]{2,1,0:T(8,128)S(1)} %get-tuple-element.448, f32[8]{0:T(128)S(1)} %fusion.88, f32[8,256]{1,0:T(8,128)S(1)} %get-tuple-element.430, f32[8,128]{1,0:T(8,128)S(1)} %get-tuple-element.431, f32[8,256]{1,0:T(8,128)S(1)} %get-tuple-element.432, ...), kind=kOutput, calls=%fused_computation.4.clone.clone.1 | convolution fusion | flops 71565312 | bytes 2396193 | tf_op jit(solution)/shard_map/while/body/eval_jaxpr/mkp,mpj->mkj/dot_general | solution.py:108
  85.7 0.3 convolution_convert_fusion.5
  86.1 1.8 %convolution_add_fusion.4 = f32[8,128,256]{2,1,0:T(8,128)S(1)} fusion(f32[8,128,256]{2,1,0:T(8,128)S(1)} %get-tuple-element.448, f32[8]{0:T(128)S(1)} %fusion.88, f32[8,256]{1,0:T(8,128)S(1)} %get-tuple-element.430, f32[8,128]{1,0:T(8,128)S(1)} %get-tuple-element.431, f32[8,256]{1,0:T(8,128)S(1)} %get-tuple-element.432, ...), kind=kOutput, calls=%fused_computation.4.clone.clone.1 | convolution fusion | flops 71565312 | bytes 2396193 | tf_op jit(solution)/shard_map/while/body/eval_jaxpr/mkp,mpj->mkj/dot_general | solution.py:108
  88.2 0.3 convolution_convert_fusion.5
  88.6 1.8 %convolution_add_fusion.4 = f32[8,128,256]{2,1,0:T(8,128)S(1)} fusion(f32[8,128,256]{2,1,0:T(8,128)S(1)} %get-tuple-element.448, f32[8]{0:T(128)S(1)} %fusion.88, f32[8,256]{1,0:T(8,128)S(1)} %get-tuple-element.430, f32[8,128]{1,0:T(8,128)S(1)} %get-tuple-element.431, f32[8,256]{1,0:T(8,128)S(1)} %get-tuple-element.432, ...), kind=kOutput, calls=%fused_computation.4.clone.clone.1 | convolution fusion | flops 71565312 | bytes 2396193 | tf_op jit(solution)/shard_map/while/body/eval_jaxpr/mkp,mpj->mkj/dot_general | solution.py:108
  90.8 0.3 convolution_convert_fusion.5
  91.2 1.8 %convolution_add_fusion.4 = f32[8,128,256]{2,1,0:T(8,128)S(1)} fusion(f32[8,128,256]{2,1,0:T(8,128)S(1)} %get-tuple-element.448, f32[8]{0:T(128)S(1)} %fusion.88, f32[8,256]{1,0:T(8,128)S(1)} %get-tuple-element.430, f32[8,128]{1,0:T(8,128)S(1)} %get-tuple-element.431, f32[8,256]{1,0:T(8,128)S(1)} %get-tuple-element.432, ...), kind=kOutput, calls=%fused_computation.4.clone.clone.1 | convolution fusion | flops 71565312 | bytes 2396193 | tf_op jit(solution)/shard_map/while/body/eval_jaxpr/mkp,mpj->mkj/dot_general | solution.py:108
  93.3 0.3 convolution_convert_fusion.5
  93.7 1.8 %convolution_add_fusion.4 = f32[8,128,256]{2,1,0:T(8,128)S(1)} fusion(f32[8,128,256]{2,1,0:T(8,128)S(1)} %get-tuple-element.448, f32[8]{0:T(128)S(1)} %fusion.88, f32[8,256]{1,0:T(8,128)S(1)} %get-tuple-element.430, f32[8,128]{1,0:T(8,128)S(1)} %get-tuple-element.431, f32[8,256]{1,0:T(8,128)S(1)} %get-tuple-element.432, ...), kind=kOutput, calls=%fused_computation.4.clone.clone.1 | convolution fusion | flops 71565312 | bytes 2396193 | tf_op jit(solution)/shard_map/while/body/eval_jaxpr/mkp,mpj->mkj/dot_general | solution.py:108
  95.8 0.3 convolution_convert_fusion.5
  96.2 1.8 %convolution_add_fusion.4 = f32[8,128,256]{2,1,0:T(8,128)S(1)} fusion(f32[8,128,256]{2,1,0:T(8,128)S(1)} %get-tuple-element.448, f32[8]{0:T(128)S(1)} %fusion.88, f32[8,256]{1,0:T(8,128)S(1)} %get-tuple-element.430, f32[8,128]{1,0:T(8,128)S(1)} %get-tuple-element.431, f32[8,256]{1,0:T(8,128)S(1)} %get-tuple-element.432, ...), kind=kOutput, calls=%fused_computation.4.clone.clone.1 | convolution fusion | flops 71565312 | bytes 2396193 | tf_op jit(solution)/shard_map/while/body/eval_jaxpr/mkp,mpj->mkj/dot_general | solution.py:108
  98.1 0.3 copy.36
  98.5 0.9 copy.51
  99.4 0.6 gather_fusion.1
  100.1 31.0 %all-reduce.2.cloned.1.call-done = f32[4,128,64]{1,2,0:T(8,128)} async-done(((f32[4,128,64]{1,2,0:T(8,128)}), f32[4,128,64]{1,2,0:T(8,128)}) %all-reduce.2.cloned.1.call-update) | async-done | bytes 131088 | tf_op jit(solution)/shard_map/psum | solution.py:131
  131.1 1.5 %gather_fusion = f32[2,128,64]{1,2,0:T(8,128)S(1)} fusion(f32[4,128,64]{1,2,0:T(8,128)} %all-reduce.2.cloned.1.call-done, s32[1024]{0:T(1024)S(1)} %pad_clamp_fusion), kind=kCustom, calls=%fused_computation | custom fusion | bytes 131080 | tf_op jit(solution)/shard_map/jit(_take)/gather | solution.py:133
  132.5 0.3 convolution_bitcast_fusion.1
  133.0 0.4 fusion.21
  133.4 1.0 copy.44
  134.4 0.2 copy.37
  134.7 1.1 convolution_add_fusion.1
  (214 shorter events, 6.3 us)
Async XLA Ops:
  7.4 22.4 %copy-start = (f32[8,64,64]{2,1,0:T(8,128)S(1)}, f32[8,64,64]{2,1,0:T(8,128)}, u32[]{:S(2)}) copy-start(f32[8,64,64]{2,1,0:T(8,128)} %param.14) | copy-start | bytes 393220
  7.4 21.8 %copy-start.2 = (bf16[8,64,128]{2,1,0:T(8,128)(2,1)S(1)}, bf16[8,64,128]{2,1,0:T(8,128)(2,1)}, u32[]{:S(2)}) copy-start(bf16[8,64,128]{2,1,0:T(8,128)(2,1)} %param.13) | copy-start | bytes 393220
  9.8 20.8 %all-to-all-start = ((s32[4,1,16]{2,1,0:T(1,128)}), s32[4,1,16]{2,1,0:T(1,128)S(1)}, u32[]{:S(2)}, u32[]{:S(2)}) async-start(s32[4,1,16]{2,1,0:T(1,128)} %bitcast), calls=%async_computation | async-start | bytes 4096 | tf_op jit(solution)/shard_map/all_to_all | solution.py:54
  29.1 1.2 copy-start.5
  29.8 7.7 %copy-start.6 = (s32[8,16]{1,0:T(8,128)S(1)}, s32[8,16]{1,0:T(8,128)}, u32[]{:S(2)}) copy-start(s32[8,16]{1,0:T(8,128)} %param.12) | copy-start | bytes 1540
  31.8 10.5 %all-to-all-start.2 = ((bf16[4,4,3,256]{3,1,2,0:T(4,128)(2,1)}), bf16[4,4,3,256]{3,1,2,0:T(4,128)(2,1)S(1)}, u32[]{:S(2)}, u32[]{:S(2)}) async-start(bf16[4,4,3,256]{3,1,2,0:T(4,128)(2,1)} %bitcast.3), calls=%async_computation.2 | async-start | bytes 49152 | tf_op jit(solution)/shard_map/all_to_all | solution.py:69
  36.6 94.4 %all-reduce.2.cloned.1.call-start = ((), (), s32[]{:S(2)}) async-start(), calls=%async_computation.4 | async-start | bytes 262144 | tf_op jit(solution)/shard_map/psum | solution.py:131
  37.7 8.4 %copy-start.8 = (s32[1,2]{1,0:T(1,128)S(1)}, s32[1,2]{1,0:T(1,128)}, u32[]{:S(2)}) copy-start(s32[1,2]{1,0:T(1,128)} %param.17) | copy-start | bytes 28
  42.3 14.3 %all-to-all-start.1 = ((bf16[4,4,128,128]{3,2,1,0:T(8,128)(2,1)}), bf16[4,4,128,128]{3,2,1,0:T(8,128)(2,1)S(1)}, u32[]{:S(2)}, u32[]{:S(2)}) async-start(bf16[4,4,128,128]{3,2,1,0:T(8,128)(2,1)} %reshape.174), calls=%async_computation.1 | async-start | bytes 1048576 | tf_op jit(solution)/shard_map/all_to_all | solution.py:68
  45.7 87.7 %reduce-scatter.4.cloned.1.call-start = ((), (), s32[]{:S(2)}) async-start(), calls=%async_computation.5 | async-start | bytes 786432
  46.1 11.0 %copy-start.7 = (s32[4,16]{1,0:T(4,128)}, s32[4,16]{1,0:T(4,128)S(1)}, u32[]{:S(2)}) copy-start(s32[4,16]{1,0:T(4,128)S(1)} %broadcast_add_fusion.1) | copy-start | bytes 772
  56.9 0.7 copy-start.3
  98.1 1.3 copy-start.4
  100.0 34.7 %copy-start.1 = (f32[8,128,128]{2,1,0:T(8,128)S(1)}, f32[8,128,128]{2,1,0:T(8,128)}, u32[]{:S(2)}) copy-start(f32[8,128,128]{2,1,0:T(8,128)} %param.10) | copy-start | bytes 1572868
Sparse Core Ops, SparseCore 0:
  40.9 90.1 all-reduce.1
Sparse Core Ops, SparseCore 1:
  99.5 6.9 reduce-scatter.3
where the time goes:
time: 145 us; the launch traced here: 143 us
  waiting for transfers between devices  44.6 us (31%)
  matrix products  37.8 us (26%)
  between operations  15.1 us (10%)
  starting transfers between devices  14.7 us (10%)
  blocking collectives  11.9 us (8%)
  local copies, waits for them, and re-layouts  8.92 us (6%)
  other arithmetic  8.63 us (6%)
  loops' own time  1.55 us (1%)
    psum x1, waiting for transfers between devices, body(): root_weight_values = lax.psum(placed, ('wide', 'narrow', 'vec'))  31 us
    dot_general x16, matrix products, scatter_step(): jnp.einsum('mkp,mpj->mkj', sources, kernel_tile.astype(jnp.bfloat16), pre...  29.4 us
    all_to_all x1, waiting for transfers between devices, body(): lax.all_to_all(send_x, 'wide', split_axis=0, concat_axis=0, tiled=True)  10.4 us
    all_gather x1, blocking collectives, body(): lax.all_gather(rounded, 'narrow', axis=0, tiled=True)  7.29 us
    all_to_all x1, starting transfers between devices, body(): lax.all_to_all(needed, 'wide', split_axis=0, concat_axis=0, tiled=True)  6.32 us
    dot_general x16, matrix products, locate(): jnp.dot(one_hot, candidates, preferred_element_type=jnp.float32)  5.08 us
    all_to_all x1, starting transfers between devices, body(): lax.all_to_all(send_pts, 'wide', split_axis=0, concat_axis=0, tiled=True)  4.84 us
    all_gather x1, blocking collectives, body(): lax.all_gather(points, 'narrow', axis=0, tiled=True)  4.6 us
  transfers between devices with their start and end apart: 5, of which 3 were waited for; matrix products, arithmetic and copies ran while one was open for 34% of the time, Pallas kernels for 0%

commit v1 on v0

v1 whole, which is shorter than its diff:
```python
import functools
import math

import jax
import jax.numpy as jnp
from jax import lax
from jax.experimental import pallas as pl
from jax.experimental.pallas import tpu as pltpu
from jax.sharding import PartitionSpec as P

SEND_CAP = 4
FEATS = 16
CHUNKS = 2

RATE = 8.660254037844386
LOG2E = math.log2(math.e)
LN2 = math.log(2.0)
SCALE = (RATE * LOG2E) ** 2
MESH = pl.DeviceIdType.MESH
HIGH = lax.Precision.HIGHEST
F32, BF16, I32 = jnp.float32, jnp.bfloat16, jnp.int32


def each(count, step):
    if count <= 8:
        for i in range(count):
            step(i)
    else:
        lax.fori_loop(0, count, lambda i, _: (step(i), 0)[1], 0)


def pieces(value):
    first = value.astype(BF16).astype(F32)
    rest = value - first
    second = rest.astype(BF16).astype(F32)
    return [first, second, rest - second]


def dot(a, b, ca=1, cb=0, precision=None):
    return lax.dot_general(
        a, b, (((ca,), (cb,)), ((), ())), precision=precision, preferred_element_type=F32
    )


def kernel(
    W, N, V,
    vec_ref, pts_ref, near_s, near_v, basis_ref, lt_ref, ptc_ref, skel_ref, coup_s,
    out_ref, *scratch,
):
    ch = CHUNKS
    loc, cand, scratch = scratch[:ch], scratch[ch : 2 * ch], scratch[2 * ch :]
    (
        stage, req_out, req_in, req_s, map_v, map_s, pts_out, pts_in, feat, bfeat, tiles,
        term, mate_in, top_all, fpiece, field, near_out, near_in, near_acc,
        s_req, r_req, s_pts, r_pts, s_nar, r_nar, s_wide, r_wide,
        s_mate, r_mate, s_top, r_top, s_ag, r_ag, s_near, r_near, l_req, l_map,
    ) = scratch
    ld, cols, half = vec_ref.shape
    full = pts_ref.shape[2]
    slots = near_v.shape[1]
    cw = cols // ch
    block = ld * N
    leaves = W * block
    shift = block.bit_length() - 1
    lp = max(128, leaves)
    mates = N * V
    pr = cols // mates
    w, n, v = lax.axis_index("wide"), lax.axis_index("narrow"), lax.axis_index("vec")
    me = n * V + v

    def mate(d):
        m = lax.rem(me + d, mates)
        return {"narrow": m // V, "vec": m % V}

    def wide_peer(d):
        return {"wide": lax.rem(w + d, W)}

    def narrow_peer(d):
        return {"narrow": lax.rem(n + d, N)}

    spot = w * N + n

    def group_peer(d):
        p = lax.rem(spot + d, W * N)
        return {"wide": p // N, "narrow": p % N}

    other = {"vec": 1 - v}

    def rcopy(src, dst, ss, rs, dev):
        return pltpu.make_async_remote_copy(
            src_ref=src, dst_ref=dst, send_sem=ss, recv_sem=rs, device_id=dev, device_id_type=MESH
        )

    barrier = pltpu.get_barrier_semaphore()

    def greet(fn):
        def step(i):
            pl.semaphore_signal(barrier, inc=1, device_id=fn(i + 1), device_id_type=MESH)
        return step

    each(W * N - 1, greet(group_peer))
    each(mates - 1, greet(mate))

    base = n * ld
    for c in range(ch):
        loc[c][pl.ds(base, ld)] = vec_ref[:, c * cw : (c + 1) * cw, :].astype(BF16)
        cand[c][pl.ds(block + w * SEND_CAP, SEND_CAP)] = jnp.zeros((SEND_CAP, cw, half), BF16)

    nl = near_v[...]
    lane = lax.broadcasted_iota(I32, (ld, lp), 1)
    hits = jnp.zeros((ld, lp), F32)
    for k in range(slots):
        hits = jnp.where(nl[:, k : k + 1] == lane, 1.0, hits)
    mask = jnp.broadcast_to(jnp.max(hits, axis=0, keepdims=True), (8, lp))
    lane8 = lax.broadcasted_iota(I32, (8, lp), 1)
    owner8 = lax.shift_right_logical(lane8, shift)
    mask = jnp.where(owner8 == w, 0.0, mask)
    ti = lax.broadcasted_iota(I32, (lp, lp), 0)
    tj = lax.broadcasted_iota(I32, (lp, lp), 1)
    tri = (ti < tj) & (lax.shift_right_logical(ti, shift) == lax.shift_right_logical(tj, shift))
    rank = dot(mask.astype(BF16), jnp.where(tri, 1.0, 0.0).astype(BF16))
    row8 = lax.broadcasted_iota(I32, (8, lp), 0).astype(F32)
    inner8 = (lane8 & (block - 1)).astype(F32)
    sel = jnp.where((rank == row8) & (mask > 0.5), inner8, 0.0)
    si = lax.broadcasted_iota(I32, (lp, 128), 0)
    sj = lax.broadcasted_iota(I32, (lp, 128), 1)
    seg = jnp.where(lax.shift_right_logical(si, shift) == sj, 1.0, 0.0).astype(BF16)
    req_out[...] = dot(sel.astype(BF16), seg).astype(I32)

    pts = pts_ref[...].astype(F32)
    xyz = [pts[:, c, :] for c in range(3)]
    halves = [jnp.where(v == 0, a[:, :half], a[:, half:]) for a in xyz]
    prow = pts_out.shape[0]
    pts_out[...] = jnp.concatenate(
        halves + [jnp.zeros((prow - 3 * ld, half), F32)], axis=0
    ).astype(BF16)
    pts_in[pl.ds(spot, 1)] = pts_out[...][None]

    weights = [
        dot(
            jnp.concatenate([loc[c][base + l] for c in range(ch)], axis=0), basis_ref[l], 1, 1
        )
        for l in range(ld)
    ]
    sums = weights[0] * 0.0
    for l in range(ld):
        sums = sums + dot(weights[l], lt_ref[l], precision=HIGH)
    term[...] = dot(sums, ptc_ref[0], precision=HIGH).reshape(mates, pr, -1)

    pl.semaphore_wait(barrier, W * N - 1 + mates - 1)

    def req_copy(i):
        return rcopy(req_out, req_in.at[i], s_req.at[i], r_req.at[i], wide_peer(i + 1))

    def mate_copy(i):
        m = lax.rem(me + i + 1, mates)
        return rcopy(term.at[m], mate_in.at[i], s_mate.at[i], r_mate.at[i], mate(i + 1))

    def pts_copy(i):
        return rcopy(pts_out, pts_in.at[spot], s_pts.at[i], r_pts.at[i], group_peer(i + 1))

    def nar_copy(i, c):
        mine = loc[c].at[pl.ds(base, ld)]
        return rcopy(mine, mine, s_nar.at[c, i], r_nar.at[c, i], narrow_peer(i + 1))

    each(W - 1, lambda i: req_copy(i).start())
    each(mates - 1, lambda i: mate_copy(i).start())
    each(W * N - 1, lambda i: pts_copy(i).start())
    for c in range(ch):
        each(N - 1, lambda i: nar_copy(i, c).start())

    owner_l = lax.shift_right_logical(lane, shift)
    place = jnp.where(
        owner_l == w,
        (lane - w * block).astype(F32),
        (block + owner_l * SEND_CAP).astype(F32) + jnp.broadcast_to(rank[:1], (ld, lp)),
    )
    mlane = lax.broadcasted_iota(I32, (ld, 128), 1)
    found = jnp.zeros((ld, 128), F32)
    zero_slot = (block + w * SEND_CAP).astype(F32)
    for k in range(slots):
        entry = nl[:, k : k + 1]
        at = jnp.sum(jnp.where(entry == lane, place, 0.0), axis=1, keepdims=True)
        at = jnp.where(entry >= 0, at, zero_slot)
        found = jnp.where(mlane == k, at, found)
    map_v[...] = found.astype(I32)
    map_copy = pltpu.make_async_copy(map_v, map_s, l_map)
    map_copy.start()

    rows = ld * FEATS
    pi = lax.broadcasted_iota(I32, (rows, rows), 0)
    pj = lax.broadcasted_iota(I32, (rows, rows), 1)
    fshift = FEATS.bit_length() - 1
    perm = pj == (pi & (FEATS - 1)) * ld + lax.shift_right_logical(pi, fshift)
    perm = jnp.where(perm, 1.0, 0.0).astype(BF16)
    one_b = jnp.ones((ld, full), F32)
    norm = (xyz[0] * xyz[0] + xyz[1] * xyz[1] + xyz[2] * xyz[2]) * SCALE
    brows = sum((pieces(a * (-2.0 * SCALE)) for a in xyz), [])
    brows = brows + [one_b] * 3 + pieces(norm) + [one_b * 0.0]
    bfeat[...] = (
        dot(perm, jnp.concatenate(brows, axis=0).astype(BF16))
        .astype(BF16)
        .reshape(ld, FEATS, full)
    )

    each(mates - 1, lambda i: mate_copy(i).wait_recv())
    mine = term[me]
    for i in range(mates - 1):
        mine = mine + mate_in[i]
    top_all[pl.ds(w, 1)] = mine[None]

    def top_copy(i):
        t = top_all.at[w]
        return rcopy(t, t, s_top.at[i], r_top.at[i], wide_peer(i + 1))

    each(W - 1, lambda i: top_copy(i).start())

    each(W - 1, lambda i: req_copy(i).wait_recv())
    req_local = pltpu.make_async_copy(req_in, req_s, l_req)
    req_local.start()
    req_local.wait()

    def wide_copy(i, c):
        return rcopy(
            stage.at[c, i], cand[c].at[pl.ds(block + w * SEND_CAP, SEND_CAP)],
            s_wide.at[c, i], r_wide.at[c, i], wide_peer(i + 1),
        )

    for c in range(ch):
        each(N - 1, lambda i: nar_copy(i, c).wait_recv())

        def put(i):
            for r in range(SEND_CAP):
                leaf = jnp.clip(req_s[i, r, w], 0, block - 1)
                stage[c, W - 2 - i, r] = loc[c][leaf]

        each(W - 1, put)
        each(W - 1, lambda i: wide_copy(i, c).start())
        cand[c][pl.ds(0, block)] = loc[c][...]

    each(W * N - 1, lambda i: pts_copy(i).wait_recv())

    def features(i):
        a = pts_in[i].astype(F32)
        abc = [a[c * ld : (c + 1) * ld] for c in range(3)]
        anorm = (abc[0] * abc[0] + abc[1] * abc[1] + abc[2] * abc[2]) * SCALE
        one_a = jnp.ones((ld, half), F32)
        arows = [abc[0]] * 3 + [abc[1]] * 3 + [abc[2]] * 3
        arows = arows + pieces(anorm) + [one_a] * 3 + [one_a * 0.0]
        feat[pl.ds(i * ld, ld)] = (
            dot(perm, jnp.concatenate(arows, axis=0).astype(BF16))
            .astype(BF16)
            .reshape(ld, FEATS, half)
        )

    each(W * N, features)

    def make_tiles(first, last):
        def step(t, carry):
            b = bfeat[t]
            for k in range(slots):
                a = feat[jnp.maximum(near_s[t, k], 0)]
                s = jnp.maximum(dot(a, b, 0, 0), 1e-30)
                q = s * lax.rsqrt(s)
                tile = (1.0 + LN2 * q) * jnp.exp2(-q)
                tiles[t, k * half : (k + 1) * half, :] = tile.astype(BF16)
            return carry

        lax.fori_loop(first, last, step, 0)

    cut = ld // 2
    make_tiles(0, cut)

    each(W - 1, lambda i: top_copy(i).wait_recv())
    rank_dim = skel_ref.shape[2]
    own = skel_ref[w]
    fields = jnp.zeros((pr, rank_dim), F32)
    for k in range(coup_s.shape[1]):
        partner = coup_s[0, k]
        src = skel_ref[partner]
        sq = jnp.zeros((rank_dim, rank_dim), F32)
        for c in range(3):
            col = jnp.broadcast_to(src[c : c + 1, :], (rank_dim, rank_dim)).T
            delta = col - own[c : c + 1, :]
            sq = sq + delta * delta
        q = RATE * jnp.sqrt(sq)
        tile = 0.125 * (1.0 + q) * jnp.exp(-q)
        fields = fields + dot(top_all[partner], tile, precision=HIGH)
    fpiece[pl.ds(me, 1)] = fields[None]

    def ag_copy(i):
        f = fpiece.at[me]
        return rcopy(f, f, s_ag.at[i], r_ag.at[i], mate(i + 1))

    each(mates - 1, lambda i: ag_copy(i).start())
    make_tiles(cut, ld)
    each(mates - 1, lambda i: ag_copy(i).wait_recv())

    top = fpiece[...].reshape(cols, rank_dim)
    parent = dot(top, ptc_ref[0], 1, 1, precision=HIGH)
    for l in range(ld):
        lf = dot(parent, lt_ref[l], 1, 1, precision=HIGH).astype(BF16)
        out_ref[l] = vec_ref[l] + dot(lf, basis_ref[l])

    map_copy.wait()

    def near_copy(c, t):
        return rcopy(
            near_out.at[c, t], near_in.at[c, t], s_near.at[c, t], r_near.at[c, t], other
        )

    for c in range(ch):
        each(W - 1, lambda i: wide_copy(i, c).wait_recv())

        def product(t, carry):
            acc = jnp.zeros((cw, full), F32)
            for k in range(0, slots, 2):
                at = [jnp.clip(map_s[t, k + j], 0, block + W * SEND_CAP - 1) for j in range(2)]
                lhs = jnp.concatenate([cand[c][at[0]], cand[c][at[1]]], axis=1)
                acc = acc + dot(lhs, tiles[t, k * half : (k + 2) * half, :])
            acc = acc * 0.125
            low, high = acc[:, :half], acc[:, half:]
            near_acc[t, c * cw : (c + 1) * cw, :] = jnp.where(v == 0, low, high)
            near_out[c, t] = jnp.where(v == 0, high, low).astype(BF16)
            near_copy(c, t).start()
            return carry

        lax.fori_loop(0, ld, product, 0)

    for c in range(ch):
        def finish(t, carry):
            near_copy(c, t).wait_recv()
            rows_c = slice(c * cw, (c + 1) * cw)
            out_ref[t, rows_c, :] = (
                out_ref[t, rows_c, :] + near_acc[t, rows_c, :] + near_in[c, t].astype(F32)
            )
            return carry

        lax.fori_loop(0, ld, finish, 0)

    each(W - 1, lambda i: req_copy(i).wait_send())
    each(mates - 1, lambda i: mate_copy(i).wait_send())
    each(W * N - 1, lambda i: pts_copy(i).wait_send())
    each(W - 1, lambda i: top_copy(i).wait_send())
    each(mates - 1, lambda i: ag_copy(i).wait_send())
    for c in range(ch):
        each(N - 1, lambda i: nar_copy(i, c).wait_send())
        each(W - 1, lambda i: wide_copy(i, c).wait_send())
        each(ld, lambda t: near_copy(c, t).wait_send())


def body(W, N, V, vectors, points, near_list, basis, transfer, ptc, skeleton, coupling):
    ld, cols, half = vectors.shape
    full = points.shape[2]
    slots = near_list.shape[1]
    rank = transfer.shape[1]
    ch = CHUNKS
    cw = cols // ch
    block = ld * N
    mates = N * V
    pr = cols // mates
    prow = -(-3 * ld // 16) * 16
    dma = pltpu.SemaphoreType.DMA
    vmem = pltpu.VMEM
    scratch = [vmem((block, cw, half), BF16)] * ch
    scratch += [vmem((block + W * SEND_CAP, cw, half), BF16)] * ch
    scratch += [
        vmem((ch, W - 1, SEND_CAP, cw, half), BF16),
        vmem((8, 128), I32),
        vmem((W - 1, 8, 128), I32),
        pltpu.SMEM((W - 1, 8, 128), I32),
        vmem((ld, 128), I32),
        pltpu.SMEM((ld, 128), I32),
        vmem((prow, half), BF16),
        vmem((W * N, prow, half), BF16),
        vmem((W * N * ld, FEATS, half), BF16),
        vmem((ld, FEATS, full), BF16),
        vmem((ld, slots * half, full), BF16),
        vmem((mates, pr, rank), F32),
        vmem((mates - 1, pr, rank), F32),
        vmem((W, pr, rank), F32),
        vmem((mates, pr, rank), F32),
        vmem((8, 128), F32),
        vmem((ch, ld, cw, half), BF16),
        vmem((ch, ld, cw, half), BF16),
        vmem((ld, cols, half), F32),
    ]
    scratch += [dma((W - 1,))] * 2 + [dma((W * N - 1,))] * 2 + [dma((ch, N - 1))] * 2
    scratch += [dma((ch, W - 1))] * 2 + [dma((mates - 1,))] * 2 + [dma((W - 1,))] * 2
    scratch += [dma((mates - 1,))] * 2 + [dma((ch, ld))] * 2 + [dma(())] * 2
    in_v = pl.BlockSpec(memory_space=pltpu.VMEM)
    in_s = pl.BlockSpec(memory_space=pltpu.SMEM)
    return pl.pallas_call(
        functools.partial(kernel, W, N, V),
        out_shape=jax.ShapeDtypeStruct(vectors.shape, F32),
        in_specs=[in_v, in_v, in_s, in_v, in_v, in_v, in_v, in_v, in_s],
        out_specs=in_v,
        scratch_shapes=scratch,
        compiler_params=pltpu.CompilerParams(
            collective_id=0, has_side_effects=True, vmem_limit_bytes=56 << 20
        ),
    )(vectors, points, near_list, near_list, basis, transfer, ptc, skeleton, coupling)


def solution(mesh):
    rows = ("groups", "wide", "narrow")
    in_specs = (
        P(rows, None, "vec"),
        P(rows, None, None),
        P(rows, None),
        P(rows, None, "vec"),
        P(rows, None, None),
        P(rows, None, None),
        P("groups", None, None),
        P(("groups", "wide"), None),
    )
    sizes = [mesh.shape[a] for a in ("wide", "narrow", "vec")]
    return jax.shard_map(
        functools.partial(body, *sizes),
        mesh=mesh,
        in_specs=in_specs,
        out_specs=P(rows, None, "vec"),
        check_vma=False,
    )
```

time: 145 us -> 36.7 us (0.25); the launches traced: 143 us -> 36.5 us
  waiting for transfers between devices: 44.6 us -> 0 us
  matrix products: 37.8 us -> 0 us
  Pallas kernels: 0 us -> 32.7 us
  between operations: 15.1 us -> 0.01 us
  starting transfers between devices: 14.7 us -> 0 us
  blocking collectives: 11.9 us -> 0 us
  other arithmetic: 8.63 us -> 0 us
  local copies, waits for them, and re-layouts: 8.92 us -> 3.79 us
  loops' own time: 1.55 us -> 0 us
    dot_general x40 -> x0, matrix products: 37.8 us -> none  [the longest x16 29.4 us: scatter_step(): jnp.einsum('mkp,mpj->mkj', sources, kernel_tile.astype(jnp.bfloat16), pre...]
    pallas_call x0 -> x1, Pallas kernels: none -> 32.7 us  [body(): pl.pallas_call(functools.partial(kernel, W, N, V), out_shape=jax.ShapeDty...]
    psum x1 -> x0, waiting for transfers between devices: 31 us -> none  [body(): root_weight_values = lax.psum(placed, ('wide', 'narrow', 'vec'))]
    all_to_all x3 -> x0, starting transfers between devices: 14.6 us -> none  [the longest x1 6.32 us: body(): lax.all_to_all(needed, 'wide', split_axis=0, concat_axis=0, tiled=True)]
    all_to_all x3 -> x0, waiting for transfers between devices: 13.6 us -> none  [the longest x1 10.4 us: body(): lax.all_to_all(send_x, 'wide', split_axis=0, concat_axis=0, tiled=True)]
    all_gather x2 -> x0, blocking collectives: 11.9 us -> none  [the longest x1 7.29 us: body(): lax.all_gather(rounded, 'narrow', axis=0, tiled=True)]
    reduce_sum x16 -> x0, other arithmetic: 2.92 us -> none  [locate(): jnp.sum((clamped[:, None] == leaf_range[None, :]).astype(jnp.int32) * nee...]
    gather x2 -> x0, local copies, waits for them, and re-layouts: 2.02 us -> none  [the longest x1 1.45 us: body(): sources_top = jnp.take(root_weight_values, partners, axis=0)]
  transfers between devices with their start and end apart: 5 -> 0, of which waited for: 3 -> 0; matrix products, arithmetic and copies ran while one was open for 34% -> 0% of each run, Pallas kernels for 0% -> 0%
where the time goes in v1:
time: 36.7 us; the launch traced here: 36.5 us
  Pallas kernels  32.7 us (89%)
  local copies, waits for them, and re-layouts  3.79 us (10%)
    pallas_call x1, Pallas kernels, body(): pl.pallas_call(functools.partial(kernel, W, N, V), out_shape=jax.ShapeDty...  32.7 us
    unnamed x5, local copies, waits for them, and re-layouts  3.79 us

profile of v1, /device:TPU:0, one launch (start us, length us, event | category | flops | bytes accessed | tf_op | source)
XLA Modules:
  0.0 36.5 jit_solution(13619530441500140165)
XLA Ops:
  0.0 0.0 copy-start
  0.0 1.3 %copy.10.skel_ref = f32[4,3,64]{2,1,0:T(4,128)} copy(f32[4,3,64]{2,0,1:T(4,128)} %param.14) | data formatting | bytes 6144 | tf_op args[6]
  1.3 0.0 copy-done
  1.3 0.6 %copy.9.pts_ref = bf16[8,3,256]{2,1,0:T(4,128)(2,1)} copy(bf16[8,3,256]{2,0,1:T(8,128)(2,1)S(1)} %copy-done) | data formatting | bytes 24576 | tf_op args[1]
  1.9 32.7 %shard_map.82 = f32[8,128,128]{2,1,0:T(8,128)} custom-call(f32[8,128,128]{2,1,0:T(8,128)} %vec_ref.1, bf16[8,3,256]{2,1,0:T(4,128)(2,1)} %copy.9.pts_ref, s32[8,16]{1,0:T(8,128)} %near_v.1, s32[8,16]{1,0:T(8,128)} %near_v.1, bf16[8,64,128]{2,1,0:T(8,128)(2,1)} %basis_ref.1, f32[8,64,64]{2,1,0:T(8,128)} %lt_ref.1, f32[1,64,64]{2,1,0:T(8,128)} %ptc_ref.1, ...), custom_call_target="tpu_custom_call" | custom-call | tf_op jit(solution)/shard_map/pallas_call | solution.py:393
  34.6 1.9 %copy.12 = f32[8,128,128]{2,1,0:T(8,128)} copy(f32[8,128,128]{2,1,0:T(8,128)} %shard_map.82) | data formatting | bytes 1048576
Async XLA Ops:
  0.0 1.3 %copy-start = (bf16[8,3,256]{2,0,1:T(8,128)(2,1)S(1)}, bf16[8,3,256]{2,0,1:T(8,128)(2,1)}, u32[]{:S(2)}) copy-start(bf16[8,3,256]{2,0,1:T(8,128)(2,1)} %param.9) | copy-start | bytes 36868

commit v2 on v1

--- a/solution.py
+++ b/solution.py
@@ -10,7 +10,7 @@
 
 SEND_CAP = 4
 FEATS = 16
-CHUNKS = 2
+CHUNKS = 4
 
 RATE = 8.660254037844386
 LOG2E = math.log2(math.e)
@@ -51,7 +51,7 @@
     loc, cand, scratch = scratch[:ch], scratch[ch : 2 * ch], scratch[2 * ch :]
     (
         stage, req_out, req_in, req_s, map_v, map_s, pts_out, pts_in, feat, bfeat, tiles,
-        term, mate_in, top_all, fpiece, field, near_out, near_in, near_acc,
+        term, mate_in, top_all, fpiece, near_out, near_in,
         s_req, r_req, s_pts, r_pts, s_nar, r_nar, s_wide, r_wide,
         s_mate, r_mate, s_top, r_top, s_ag, r_ag, s_near, r_near, l_req, l_map,
     ) = scratch
@@ -127,8 +127,7 @@
     seg = jnp.where(lax.shift_right_logical(si, shift) == sj, 1.0, 0.0).astype(BF16)
     req_out[...] = dot(sel.astype(BF16), seg).astype(I32)
 
-    pts = pts_ref[...].astype(F32)
-    xyz = [pts[:, c, :] for c in range(3)]
+    xyz = [pts_ref[c].astype(F32) for c in range(3)]
     halves = [jnp.where(v == 0, a[:, :half], a[:, half:]) for a in xyz]
     prow = pts_out.shape[0]
     pts_out[...] = jnp.concatenate(
@@ -218,25 +217,6 @@
     each(W - 1, lambda i: req_copy(i).wait_recv())
     req_local = pltpu.make_async_copy(req_in, req_s, l_req)
     req_local.start()
-    req_local.wait()
-
-    def wide_copy(i, c):
-        return rcopy(
-            stage.at[c, i], cand[c].at[pl.ds(block + w * SEND_CAP, SEND_CAP)],
-            s_wide.at[c, i], r_wide.at[c, i], wide_peer(i + 1),
-        )
-
-    for c in range(ch):
-        each(N - 1, lambda i: nar_copy(i, c).wait_recv())
-
-        def put(i):
-            for r in range(SEND_CAP):
-                leaf = jnp.clip(req_s[i, r, w], 0, block - 1)
-                stage[c, W - 2 - i, r] = loc[c][leaf]
-
-        each(W - 1, put)
-        each(W - 1, lambda i: wide_copy(i, c).start())
-        cand[c][pl.ds(0, block)] = loc[c][...]
 
     each(W * N - 1, lambda i: pts_copy(i).wait_recv())
 
@@ -254,6 +234,13 @@
         )
 
     each(W * N, features)
+    req_local.wait()
+
+    def wide_copy(i, c):
+        return rcopy(
+            stage.at[c, i], cand[c].at[pl.ds(block + w * SEND_CAP, SEND_CAP)],
+            s_wide.at[c, i], r_wide.at[c, i], wide_peer(i + 1),
+        )
 
     def make_tiles(first, last):
         def step(t, carry):
@@ -268,34 +255,43 @@
 
         lax.fori_loop(first, last, step, 0)
 
-    cut = ld // 2
-    make_tiles(0, cut)
-
-    each(W - 1, lambda i: top_copy(i).wait_recv())
     rank_dim = skel_ref.shape[2]
-    own = skel_ref[w]
-    fields = jnp.zeros((pr, rank_dim), F32)
-    for k in range(coup_s.shape[1]):
-        partner = coup_s[0, k]
-        src = skel_ref[partner]
-        sq = jnp.zeros((rank_dim, rank_dim), F32)
-        for c in range(3):
-            col = jnp.broadcast_to(src[c : c + 1, :], (rank_dim, rank_dim)).T
-            delta = col - own[c : c + 1, :]
-            sq = sq + delta * delta
-        q = RATE * jnp.sqrt(sq)
-        tile = 0.125 * (1.0 + q) * jnp.exp(-q)
-        fields = fields + dot(top_all[partner], tile, precision=HIGH)
-    fpiece[pl.ds(me, 1)] = fields[None]
 
     def ag_copy(i):
         f = fpiece.at[me]
         return rcopy(f, f, s_ag.at[i], r_ag.at[i], mate(i + 1))
 
-    each(mates - 1, lambda i: ag_copy(i).start())
-    make_tiles(cut, ld)
+    for c in range(ch):
+        each(N - 1, lambda i: nar_copy(i, c).wait_recv())
+
+        def put(i):
+            for r in range(SEND_CAP):
+                leaf = jnp.clip(req_s[i, r, w], 0, block - 1)
+                stage[c, W - 2 - i, r] = loc[c][leaf]
+
+        each(W - 1, put)
+        each(W - 1, lambda i: wide_copy(i, c).start())
+        cand[c][pl.ds(0, block)] = loc[c][...]
+        make_tiles(c * ld // ch, (c + 1) * ld // ch)
+        if c != ch // 2:
+            continue
+
+        each(W - 1, lambda i: top_copy(i).wait_recv())
+        fields = jnp.zeros((pr, rank_dim), F32)
+        for k in range(coup_s.shape[1]):
+            partner = coup_s[0, k]
+            sq = jnp.zeros((rank_dim, rank_dim), F32)
+            for x in range(3):
+                row = skel_ref[x, pl.ds(partner, 1), :]
+                delta = jnp.broadcast_to(row, (rank_dim, rank_dim)).T - skel_ref[x, pl.ds(w, 1), :]
+                sq = sq + delta * delta
+            q = RATE * jnp.sqrt(sq)
+            tile = 0.125 * (1.0 + q) * jnp.exp(-q)
+            fields = fields + dot(top_all[partner], tile, precision=HIGH)
+        fpiece[pl.ds(me, 1)] = fields[None]
+        each(mates - 1, lambda i: ag_copy(i).start())
+
     each(mates - 1, lambda i: ag_copy(i).wait_recv())
-
     top = fpiece[...].reshape(cols, rank_dim)
     parent = dot(top, ptc_ref[0], 1, 1, precision=HIGH)
     for l in range(ld):
@@ -304,49 +300,45 @@
 
     map_copy.wait()
 
-    def near_copy(c, t):
-        return rcopy(
-            near_out.at[c, t], near_in.at[c, t], s_near.at[c, t], r_near.at[c, t], other
-        )
+    def near_copy(t):
+        return rcopy(near_out.at[t], near_in.at[t], s_near.at[t], r_near.at[t], other)
 
     for c in range(ch):
         each(W - 1, lambda i: wide_copy(i, c).wait_recv())
 
-        def product(t, carry):
-            acc = jnp.zeros((cw, full), F32)
-            for k in range(0, slots, 2):
-                at = [jnp.clip(map_s[t, k + j], 0, block + W * SEND_CAP - 1) for j in range(2)]
-                lhs = jnp.concatenate([cand[c][at[0]], cand[c][at[1]]], axis=1)
-                acc = acc + dot(lhs, tiles[t, k * half : (k + 2) * half, :])
-            acc = acc * 0.125
-            low, high = acc[:, :half], acc[:, half:]
-            near_acc[t, c * cw : (c + 1) * cw, :] = jnp.where(v == 0, low, high)
-            near_out[c, t] = jnp.where(v == 0, high, low).astype(BF16)
-            near_copy(c, t).start()
-            return carry
-
-        lax.fori_loop(0, ld, product, 0)
-
-    for c in range(ch):
-        def finish(t, carry):
-            near_copy(c, t).wait_recv()
-            rows_c = slice(c * cw, (c + 1) * cw)
-            out_ref[t, rows_c, :] = (
-                out_ref[t, rows_c, :] + near_acc[t, rows_c, :] + near_in[c, t].astype(F32)
+    def product(t, carry):
+        acc = jnp.zeros((cols, full), F32)
+        for k in range(0, slots, 2):
+            at = [jnp.clip(map_s[t, k + j], 0, block + W * SEND_CAP - 1) for j in range(2)]
+            lhs = jnp.concatenate(
+                [jnp.concatenate([cand[c][a] for c in range(ch)], axis=0) for a in at], axis=1
             )
-            return carry
-
-        lax.fori_loop(0, ld, finish, 0)
+            acc = acc + dot(lhs, tiles[t, k * half : (k + 2) * half, :])
+        acc = acc * 0.125
+        low, high = acc[:, :half], acc[:, half:]
+        near_out[t] = jnp.where(v == 0, high, low).astype(BF16)
+        near_copy(t).start()
+        out_ref[t] = out_ref[t] + jnp.where(v == 0, low, high)
+        return carry
+
+    lax.fori_loop(0, ld, product, 0)
+
+    def finish(t, carry):
+        near_copy(t).wait_recv()
+        out_ref[t] = out_ref[t] + near_in[t].astype(F32)
+        return carry
+
+    lax.fori_loop(0, ld, finish, 0)
 
     each(W - 1, lambda i: req_copy(i).wait_send())
     each(mates - 1, lambda i: mate_copy(i).wait_send())
     each(W * N - 1, lambda i: pts_copy(i).wait_send())
     each(W - 1, lambda i: top_copy(i).wait_send())
     each(mates - 1, lambda i: ag_copy(i).wait_send())
+    each(ld, lambda t: near_copy(t).wait_send())
     for c in range(ch):
         each(N - 1, lambda i: nar_copy(i, c).wait_send())
         each(W - 1, lambda i: wide_copy(i, c).wait_send())
-        each(ld, lambda t: near_copy(c, t).wait_send())
 
 
 def body(W, N, V, vectors, points, near_list, basis, transfer, ptc, skeleton, coupling):
@@ -380,14 +372,12 @@
         vmem((mates - 1, pr, rank), F32),
         vmem((W, pr, rank), F32),
         vmem((mates, pr, rank), F32),
-        vmem((8, 128), F32),
-        vmem((ch, ld, cw, half), BF16),
-        vmem((ch, ld, cw, half), BF16),
-        vmem((ld, cols, half), F32),
+        vmem((ld, cols, half), BF16),
+        vmem((ld, cols, half), BF16),
     ]
     scratch += [dma((W - 1,))] * 2 + [dma((W * N - 1,))] * 2 + [dma((ch, N - 1))] * 2
     scratch += [dma((ch, W - 1))] * 2 + [dma((mates - 1,))] * 2 + [dma((W - 1,))] * 2
-    scratch += [dma((mates - 1,))] * 2 + [dma((ch, ld))] * 2 + [dma(())] * 2
+    scratch += [dma((mates - 1,))] * 2 + [dma((ld,))] * 2 + [dma(())] * 2
     in_v = pl.BlockSpec(memory_space=pltpu.VMEM)
     in_s = pl.BlockSpec(memory_space=pltpu.SMEM)
     return pl.pallas_call(
@@ -399,7 +389,10 @@
         compiler_params=pltpu.CompilerParams(
             collective_id=0, has_side_effects=True, vmem_limit_bytes=56 << 20
         ),
-    )(vectors, points, near_list, near_list, basis, transfer, ptc, skeleton, coupling)
+    )(
+        vectors, points.transpose(1, 0, 2), near_list, near_list, basis, transfer, ptc,
+        skeleton.transpose(1, 0, 2), coupling,
+    )
 
 
 def solution(mesh):

time: 36.7 us -> 31.6 us (0.86)
  Pallas kernels: 32.7 us -> 29.6 us
  local copies, waits for them, and re-layouts: 3.79 us -> 1.87 us
    pallas_call x1, Pallas kernels: 32.7 us -> 29.6 us  [body(): pl.pallas_call(functools.partial(kernel, W, N, V), out_shape=jax.ShapeDty...]
    unnamed x5 -> x1, local copies, waits for them, and re-layouts: 3.79 us -> 1.87 us
where the time goes in v2:
time: 31.6 us; the launch traced here: 31.5 us
  Pallas kernels  29.6 us (94%)
  local copies, waits for them, and re-layouts  1.87 us (6%)
    pallas_call x1, Pallas kernels, body(): pl.pallas_call(functools.partial(kernel, W, N, V), out_shape=jax.ShapeDty...  29.6 us
    unnamed x1, local copies, waits for them, and re-layouts  1.87 us

profile of v2, /device:TPU:0, one launch (start us, length us, event | category | flops | bytes accessed | tf_op | source)
XLA Modules:
  0.0 31.5 jit_solution(4372160630045818182)
XLA Ops:
  0.0 29.6 %shard_map.82 = f32[8,128,128]{2,1,0:T(8,128)} custom-call(f32[8,128,128]{2,1,0:T(8,128)} %vec_ref.1, bf16[3,8,256]{2,1,0:T(8,128)(2,1)} %bitcast.2, s32[8,16]{1,0:T(8,128)} %near_v.1, s32[8,16]{1,0:T(8,128)} %near_v.1, bf16[8,64,128]{2,1,0:T(8,128)(2,1)} %basis_ref.1, f32[8,64,64]{2,1,0:T(8,128)} %lt_ref.1, f32[1,64,64]{2,1,0:T(8,128)} %ptc_ref.1, ...), custom_call_target="tpu_custom_call" | custom-call | tf_op jit(solution)/shard_map/pallas_call | solution.py:383
  29.6 1.9 %copy.10 = f32[8,128,128]{2,1,0:T(8,128)} copy(f32[8,128,128]{2,1,0:T(8,128)} %shard_map.82) | data formatting | bytes 1048576

commit v3 on v2

--- a/solution.py
+++ b/solution.py
@@ -168,39 +168,9 @@
     for c in range(ch):
         each(N - 1, lambda i: nar_copy(i, c).start())
 
-    owner_l = lax.shift_right_logical(lane, shift)
-    place = jnp.where(
-        owner_l == w,
-        (lane - w * block).astype(F32),
-        (block + owner_l * SEND_CAP).astype(F32) + jnp.broadcast_to(rank[:1], (ld, lp)),
-    )
-    mlane = lax.broadcasted_iota(I32, (ld, 128), 1)
-    found = jnp.zeros((ld, 128), F32)
-    zero_slot = (block + w * SEND_CAP).astype(F32)
-    for k in range(slots):
-        entry = nl[:, k : k + 1]
-        at = jnp.sum(jnp.where(entry == lane, place, 0.0), axis=1, keepdims=True)
-        at = jnp.where(entry >= 0, at, zero_slot)
-        found = jnp.where(mlane == k, at, found)
-    map_v[...] = found.astype(I32)
-    map_copy = pltpu.make_async_copy(map_v, map_s, l_map)
-    map_copy.start()
-
-    rows = ld * FEATS
-    pi = lax.broadcasted_iota(I32, (rows, rows), 0)
-    pj = lax.broadcasted_iota(I32, (rows, rows), 1)
-    fshift = FEATS.bit_length() - 1
-    perm = pj == (pi & (FEATS - 1)) * ld + lax.shift_right_logical(pi, fshift)
-    perm = jnp.where(perm, 1.0, 0.0).astype(BF16)
-    one_b = jnp.ones((ld, full), F32)
-    norm = (xyz[0] * xyz[0] + xyz[1] * xyz[1] + xyz[2] * xyz[2]) * SCALE
-    brows = sum((pieces(a * (-2.0 * SCALE)) for a in xyz), [])
-    brows = brows + [one_b] * 3 + pieces(norm) + [one_b * 0.0]
-    bfeat[...] = (
-        dot(perm, jnp.concatenate(brows, axis=0).astype(BF16))
-        .astype(BF16)
-        .reshape(ld, FEATS, full)
-    )
+    each(W - 1, lambda i: req_copy(i).wait_recv())
+    req_local = pltpu.make_async_copy(req_in, req_s, l_req)
+    req_local.start()
 
     each(mates - 1, lambda i: mate_copy(i).wait_recv())
     mine = term[me]
@@ -214,26 +184,6 @@
 
     each(W - 1, lambda i: top_copy(i).start())
 
-    each(W - 1, lambda i: req_copy(i).wait_recv())
-    req_local = pltpu.make_async_copy(req_in, req_s, l_req)
-    req_local.start()
-
-    each(W * N - 1, lambda i: pts_copy(i).wait_recv())
-
-    def features(i):
-        a = pts_in[i].astype(F32)
-        abc = [a[c * ld : (c + 1) * ld] for c in range(3)]
-        anorm = (abc[0] * abc[0] + abc[1] * abc[1] + abc[2] * abc[2]) * SCALE
-        one_a = jnp.ones((ld, half), F32)
-        arows = [abc[0]] * 3 + [abc[1]] * 3 + [abc[2]] * 3
-        arows = arows + pieces(anorm) + [one_a] * 3 + [one_a * 0.0]
-        feat[pl.ds(i * ld, ld)] = (
-            dot(perm, jnp.concatenate(arows, axis=0).astype(BF16))
-            .astype(BF16)
-            .reshape(ld, FEATS, half)
-        )
-
-    each(W * N, features)
     req_local.wait()
 
     def wide_copy(i, c):
@@ -261,6 +211,59 @@
         f = fpiece.at[me]
         return rcopy(f, f, s_ag.at[i], r_ag.at[i], mate(i + 1))
 
+    def prepare():
+        owner_l = lax.shift_right_logical(lane, shift)
+        place = jnp.where(
+            owner_l == w,
+            (lane - w * block).astype(F32),
+            (block + owner_l * SEND_CAP).astype(F32) + jnp.broadcast_to(rank[:1], (ld, lp)),
+        )
+        mlane = lax.broadcasted_iota(I32, (ld, 128), 1)
+        found = jnp.zeros((ld, 128), F32)
+        zero_slot = (block + w * SEND_CAP).astype(F32)
+        for k in range(slots):
+            entry = nl[:, k : k + 1]
+            at = jnp.sum(jnp.where(entry == lane, place, 0.0), axis=1, keepdims=True)
+            at = jnp.where(entry >= 0, at, zero_slot)
+            found = jnp.where(mlane == k, at, found)
+        map_v[...] = found.astype(I32)
+        map_copy = pltpu.make_async_copy(map_v, map_s, l_map)
+        map_copy.start()
+
+        rows = ld * FEATS
+        pi = lax.broadcasted_iota(I32, (rows, rows), 0)
+        pj = lax.broadcasted_iota(I32, (rows, rows), 1)
+        fshift = FEATS.bit_length() - 1
+        perm = pj == (pi & (FEATS - 1)) * ld + lax.shift_right_logical(pi, fshift)
+        perm = jnp.where(perm, 1.0, 0.0).astype(BF16)
+        one_b = jnp.ones((ld, full), F32)
+        norm = (xyz[0] * xyz[0] + xyz[1] * xyz[1] + xyz[2] * xyz[2]) * SCALE
+        brows = sum((pieces(a * (-2.0 * SCALE)) for a in xyz), [])
+        brows = brows + [one_b] * 3 + pieces(norm) + [one_b * 0.0]
+        bfeat[...] = (
+            dot(perm, jnp.concatenate(brows, axis=0).astype(BF16))
+            .astype(BF16)
+            .reshape(ld, FEATS, full)
+        )
+
+        each(W * N - 1, lambda i: pts_copy(i).wait_recv())
+
+        def features(i):
+            a = pts_in[i].astype(F32)
+            abc = [a[c * ld : (c + 1) * ld] for c in range(3)]
+            anorm = (abc[0] * abc[0] + abc[1] * abc[1] + abc[2] * abc[2]) * SCALE
+            one_a = jnp.ones((ld, half), F32)
+            arows = [abc[0]] * 3 + [abc[1]] * 3 + [abc[2]] * 3
+            arows = arows + pieces(anorm) + [one_a] * 3 + [one_a * 0.0]
+            feat[pl.ds(i * ld, ld)] = (
+                dot(perm, jnp.concatenate(arows, axis=0).astype(BF16))
+                .astype(BF16)
+                .reshape(ld, FEATS, half)
+            )
+
+        each(W * N, features)
+        return map_copy
+
     for c in range(ch):
         each(N - 1, lambda i: nar_copy(i, c).wait_recv())
 
@@ -271,6 +274,8 @@
 
         each(W - 1, put)
         each(W - 1, lambda i: wide_copy(i, c).start())
+        if c == 0:
+            map_copy = prepare()
         cand[c][pl.ds(0, block)] = loc[c][...]
         make_tiles(c * ld // ch, (c + 1) * ld // ch)
         if c != ch // 2:
@@ -382,7 +387,7 @@
     in_s = pl.BlockSpec(memory_space=pltpu.SMEM)
     return pl.pallas_call(
         functools.partial(kernel, W, N, V),
-        out_shape=jax.ShapeDtypeStruct(vectors.shape, F32),
+        out_shape=pltpu.VMEM(vectors.shape, F32),
         in_specs=[in_v, in_v, in_s, in_v, in_v, in_v, in_v, in_v, in_s],
         out_specs=in_v,
         scratch_shapes=scratch,

time: 31.6 us -> 29.7 us (0.940)
  local copies, waits for them, and re-layouts: 1.87 us -> 0.8 us
  Pallas kernels: 29.6 us -> 28.8 us
    unnamed x1, local copies, waits for them, and re-layouts: 1.87 us -> 0.8 us
    pallas_call x1, Pallas kernels: 29.6 us -> 28.8 us  [body(): pl.pallas_call(functools.partial(kernel, W, N, V), out_shape=pltpu.VMEM(v...]
where the time goes in v3:
time: 29.7 us; the launch traced here: 29.6 us
  Pallas kernels  28.8 us (97%)
  local copies, waits for them, and re-layouts  0.8 us (3%)
    pallas_call x1, Pallas kernels, body(): pl.pallas_call(functools.partial(kernel, W, N, V), out_shape=pltpu.VMEM(v...  28.8 us
    unnamed x1, local copies, waits for them, and re-layouts  0.8 us

profile of v3, /device:TPU:0, one launch (start us, length us, event | category | flops | bytes accessed | tf_op | source)
XLA Modules:
  0.0 29.6 jit_solution(16929330434527605489)
XLA Ops:
  0.0 28.8 %shard_map.82 = f32[8,128,128]{2,1,0:T(8,128)S(1)} custom-call(f32[8,128,128]{2,1,0:T(8,128)} %vec_ref.1, bf16[3,8,256]{2,1,0:T(8,128)(2,1)} %bitcast.2, s32[8,16]{1,0:T(8,128)} %near_v.1, s32[8,16]{1,0:T(8,128)} %near_v.1, bf16[8,64,128]{2,1,0:T(8,128)(2,1)} %basis_ref.1, f32[8,64,64]{2,1,0:T(8,128)} %lt_ref.1, f32[1,64,64]{2,1,0:T(8,128)} %ptc_ref.1, ...), custom_call_target="tpu_custom_call" | custom-call | tf_op jit(solution)/shard_map/pallas_call | solution.py:388
  28.8 0.8 %copy.10 = f32[8,128,128]{2,1,0:T(8,128)} copy(f32[8,128,128]{2,1,0:T(8,128)S(1)} %shard_map.82) | data formatting | bytes 1048576

commit v4 on v3

--- a/solution.py
+++ b/solution.py
@@ -44,16 +44,17 @@
 
 def kernel(
     W, N, V,
-    vec_ref, pts_ref, near_s, near_v, basis_ref, lt_ref, ptc_ref, skel_ref, coup_s,
-    out_ref, *scratch,
+    *refs,
 ):
     ch = CHUNKS
+    args, out_ref, here, scratch = refs[:9], refs[9], refs[10:19], refs[19:]
+    vec_ref, pts_ref, near_s, near_v, basis_ref, lt_ref, ptc_ref, skel_ref, coup_s = here
     loc, cand, scratch = scratch[:ch], scratch[ch : 2 * ch], scratch[2 * ch :]
     (
         stage, req_out, req_in, req_s, map_v, map_s, pts_out, pts_in, feat, bfeat, tiles,
         term, mate_in, top_all, fpiece, near_out, near_in,
         s_req, r_req, s_pts, r_pts, s_nar, r_nar, s_wide, r_wide,
-        s_mate, r_mate, s_top, r_top, s_ag, r_ag, s_near, r_near, l_req, l_map,
+        s_mate, r_mate, s_top, r_top, s_ag, r_ag, s_near, r_near, l_req, l_map, l_in,
     ) = scratch
     ld, cols, half = vec_ref.shape
     full = pts_ref.shape[2]
@@ -101,11 +102,17 @@
     each(W * N - 1, greet(group_peer))
     each(mates - 1, greet(mate))
 
+    fetch = [pltpu.make_async_copy(a, h, l_in.at[i]) for i, (a, h) in enumerate(zip(args, here))]
+    for i in (3, 0, 1, 4, 5, 6, 2, 7, 8):
+        fetch[i].start()
+    fetch[0].wait()
+
     base = n * ld
     for c in range(ch):
         loc[c][pl.ds(base, ld)] = vec_ref[:, c * cw : (c + 1) * cw, :].astype(BF16)
         cand[c][pl.ds(block + w * SEND_CAP, SEND_CAP)] = jnp.zeros((SEND_CAP, cw, half), BF16)
 
+    fetch[3].wait()
     nl = near_v[...]
     lane = lax.broadcasted_iota(I32, (ld, lp), 1)
     hits = jnp.zeros((ld, lp), F32)
@@ -127,6 +134,7 @@
     seg = jnp.where(lax.shift_right_logical(si, shift) == sj, 1.0, 0.0).astype(BF16)
     req_out[...] = dot(sel.astype(BF16), seg).astype(I32)
 
+    fetch[1].wait()
     xyz = [pts_ref[c].astype(F32) for c in range(3)]
     halves = [jnp.where(v == 0, a[:, :half], a[:, half:]) for a in xyz]
     prow = pts_out.shape[0]
@@ -135,6 +143,8 @@
     ).astype(BF16)
     pts_in[pl.ds(spot, 1)] = pts_out[...][None]
 
+    for i in (4, 5, 6, 2, 7, 8):
+        fetch[i].wait()
     weights = [
         dot(
             jnp.concatenate([loc[c][base + l] for c in range(ch)], axis=0), basis_ref[l], 1, 1
@@ -359,7 +369,14 @@
     prow = -(-3 * ld // 16) * 16
     dma = pltpu.SemaphoreType.DMA
     vmem = pltpu.VMEM
-    scratch = [vmem((block, cw, half), BF16)] * ch
+    operands = (
+        vectors, points.transpose(1, 0, 2), near_list, near_list, basis, transfer, ptc,
+        skeleton.transpose(1, 0, 2), coupling,
+    )
+    scratch = [
+        (pltpu.SMEM if i in (2, 8) else vmem)(a.shape, a.dtype) for i, a in enumerate(operands)
+    ]
+    scratch += [vmem((block, cw, half), BF16)] * ch
     scratch += [vmem((block + W * SEND_CAP, cw, half), BF16)] * ch
     scratch += [
         vmem((ch, W - 1, SEND_CAP, cw, half), BF16),
@@ -382,22 +399,17 @@
     ]
     scratch += [dma((W - 1,))] * 2 + [dma((W * N - 1,))] * 2 + [dma((ch, N - 1))] * 2
     scratch += [dma((ch, W - 1))] * 2 + [dma((mates - 1,))] * 2 + [dma((W - 1,))] * 2
-    scratch += [dma((mates - 1,))] * 2 + [dma((ld,))] * 2 + [dma(())] * 2
-    in_v = pl.BlockSpec(memory_space=pltpu.VMEM)
-    in_s = pl.BlockSpec(memory_space=pltpu.SMEM)
+    scratch += [dma((mates - 1,))] * 2 + [dma((ld,))] * 2 + [dma(())] * 2 + [dma((9,))]
     return pl.pallas_call(
         functools.partial(kernel, W, N, V),
         out_shape=pltpu.VMEM(vectors.shape, F32),
-        in_specs=[in_v, in_v, in_s, in_v, in_v, in_v, in_v, in_v, in_s],
-        out_specs=in_v,
+        in_specs=[pl.BlockSpec(memory_space=pl.ANY)] * 9,
+        out_specs=pl.BlockSpec(memory_space=pltpu.VMEM),
         scratch_shapes=scratch,
         compiler_params=pltpu.CompilerParams(
             collective_id=0, has_side_effects=True, vmem_limit_bytes=56 << 20
         ),
-    )(
-        vectors, points.transpose(1, 0, 2), near_list, near_list, basis, transfer, ptc,
-        skeleton.transpose(1, 0, 2), coupling,
-    )
+    )(*operands)
 
 
 def solution(mesh):

time: 29.7 us -> 29.3 us (0.987)
  Pallas kernels: 28.8 us -> 28.4 us
    pallas_call x1, Pallas kernels: 28.8 us -> 28.4 us  [body(): pl.pallas_call(functools.partial(kernel, W, N, V), out_shape=pltpu.VMEM(v...]
where the time goes in v4:
time: 29.3 us; the launch traced here: 29.2 us
  Pallas kernels  28.4 us (97%)
  local copies, waits for them, and re-layouts  0.8 us (3%)
    pallas_call x1, Pallas kernels, body(): pl.pallas_call(functools.partial(kernel, W, N, V), out_shape=pltpu.VMEM(v...  28.4 us
    unnamed x1, local copies, waits for them, and re-layouts  0.8 us

profile of v4, /device:TPU:0, one launch (start us, length us, event | category | flops | bytes accessed | tf_op | source)
XLA Modules:
  0.0 29.2 jit_solution(13752525905898267631)
XLA Ops:
  0.0 28.4 %shard_map.82 = f32[8,128,128]{2,1,0:T(8,128)S(1)} custom-call(f32[8,128,128]{2,1,0:T(8,128)} %refs_0_.1, bf16[3,8,256]{2,1,0:T(8,128)(2,1)} %bitcast.2, s32[8,16]{1,0:T(8,128)} %refs_3_.1, s32[8,16]{1,0:T(8,128)} %refs_3_.1, bf16[8,64,128]{2,1,0:T(8,128)(2,1)} %refs_4_.1, f32[8,64,64]{2,1,0:T(8,128)} %refs_5_.1, f32[1,64,64]{2,1,0:T(8,128)} %refs_6_.1, ...), custom_call_target="tpu_custom_call" | custom-call | tf_op jit(solution)/shard_map/pallas_call | solution.py:403
  28.4 0.8 %copy.10 = f32[8,128,128]{2,1,0:T(8,128)} copy(f32[8,128,128]{2,1,0:T(8,128)S(1)} %shard_map.82) | data formatting | bytes 1048576
